TPU v7x, 256 devices: a whole 4x4x8 slice. The times are simulated.
256 devices in a mesh: seq: 32 (over z, x), req: 8 (over y, core).
Axes of the slice: x: 4, y: 4, z: 8, core: 2. Of those that a mesh axis runs over, the one named last changes fastest.
Arguments:
- tokens: bfloat16 [64, 4, 2048], P('req'), may hold values from -6 to 6
- lengths: int32 [64], P('req'), may hold values from 1 to 2044, as said below
- cache_keys: bfloat16 [64, 2048, 2048], P('req', 'seq'), may hold values from -120 to 120
- cache_values: bfloat16 [64, 2048, 2048], P('req', 'seq'), may hold values from -6 to 6
- norm1_gain: float32 [2048], replicated, may hold values from 0.5 to 1.5
- norm1_bias: float32 [2048], replicated, may hold values from -1.75 to 1.75
- w_query: bfloat16 [2048, 2048], P('req', 'seq'), may hold values from -0.125 to 0.125
- b_query: float32 [2048], P('seq'), may hold values from -3 to 3
- w_key: bfloat16 [2048, 2048], P('req', 'seq'), may hold values from -0.125 to 0.125
- b_key: float32 [2048], P('seq'), may hold values from -3 to 3
- w_value: bfloat16 [2048, 2048], P('req', 'seq'), may hold values from -0.125 to 0.125
- b_value: float32 [2048], P('seq'), may hold values from -3 to 3
- w_out: bfloat16 [2048, 2048], P('req', 'seq'), may hold values from -0.125 to 0.125
- b_out: float32 [2048], P('seq'), may hold values from -3 to 3
- norm2_gain: float32 [2048], replicated, may hold values from 0.5 to 1.5
- norm2_bias: float32 [2048], replicated, may hold values from -1.75 to 1.75
- w_up: bfloat16 [2048, 8192], P('req', 'seq'), may hold values from -0.125 to 0.125
- b_up: float32 [8192], P('seq'), may hold values from -3 to 3
- w_down: bfloat16 [8192, 2048], P('seq', 'req'), may hold values from -0.0625 to 0.0625
- b_down: float32 [2048], replicated, may hold values from -3 to 3
Outputs:
- hidden_out: bfloat16 [64, 4, 2048], P('req')
- new_keys: bfloat16 [64, 2048, 2048], P('req', 'seq')
- new_values: bfloat16 [64, 2048, 2048], P('req', 'seq')
Inputs may be any that keep to these rules, and one draw needn't show every extreme that they name: `lengths`: one request has exactly 2044 cached positions.
All inputs are finite; a program needn't handle non-finite values.
Results may differ from a plain program's by a relative error of at most 0.033.
Values may be sent and summed in bfloat16 or wider, within the bound.
A program may use at most 64 MiB of HBM per device.

v0:
```python
import jax
import jax.numpy as jnp
from jax import lax
from jax.sharding import PartitionSpec as P

HEADS = 16
HEAD = 128


def merged(x, axis, combine):
    everything = jax.tree.map(
        lambda part, kind: lax.all_gather(part.astype(kind), axis),
        x,
        (jnp.bfloat16, jnp.bfloat16, jnp.bfloat16),
    )

    def take(k):
        return jax.tree.map(lambda part, own: part[k].astype(own.dtype), everything, x)

    return lax.fori_loop(
        1, lax.axis_size(axis), lambda k, so_far: combine(so_far, take(k)), take(0)
    )


def layer_norm(values, gain, shift):
    center = values - jnp.mean(values, axis=-1, keepdims=True)
    spread = jnp.mean(center * center, axis=-1, keepdims=True)
    return center * lax.rsqrt(spread + 1e-05) * gain + shift


def combine(first, second):
    peak_a, total_a, part_a = first
    peak_b, total_b, part_b = second
    peak = jnp.maximum(peak_a, peak_b)
    scale_a = jnp.exp(peak_a - peak)
    scale_b = jnp.exp(peak_b - peak)
    total = total_a * scale_a + total_b * scale_b
    part = part_a * scale_a[..., None] + part_b * scale_b[..., None]
    return (peak, total, part)


def body(
    tokens,
    lengths,
    cache_keys,
    cache_values,
    norm1_gain,
    norm1_bias,
    w_query,
    b_query,
    w_key,
    b_key,
    w_value,
    b_value,
    w_out,
    b_out,
    norm2_gain,
    norm2_bias,
    w_up,
    b_up,
    w_down,
    b_down,
):
    group = tokens.shape[0]
    residual = tokens.astype(jnp.float32)
    normed = layer_norm(residual, norm1_gain, norm1_bias).astype(jnp.bfloat16)
    full_query, full_key, full_value, full_out, full_up = (
        lax.all_gather(w_query, "req", axis=0, tiled=True),
        lax.all_gather(w_key, "req", axis=0, tiled=True),
        lax.all_gather(w_value, "req", axis=0, tiled=True),
        lax.all_gather(w_out, "req", axis=0, tiled=True),
        lax.all_gather(w_up, "req", axis=0, tiled=True),
    )
    query_cols = (jnp.dot(normed, full_query, preferred_element_type=jnp.float32) + b_query).astype(
        jnp.bfloat16
    )
    key_cols = (jnp.dot(normed, full_key, preferred_element_type=jnp.float32) + b_key).astype(
        jnp.bfloat16
    )
    value_cols = (jnp.dot(normed, full_value, preferred_element_type=jnp.float32) + b_value).astype(
        jnp.bfloat16
    )
    query, key_rows, value_rows = (
        lax.all_gather(query_cols, "seq", axis=2, tiled=True),
        lax.all_gather(key_cols, "seq", axis=2, tiled=True),
        lax.all_gather(value_cols, "seq", axis=2, tiled=True),
    )
    steps, width = (query.shape[1], query.shape[2])
    slots = cache_keys.shape[1]
    position = lax.axis_index("seq") * slots + jnp.arange(slots, dtype=jnp.int32)
    new_keys = cache_keys
    new_values = cache_values
    for step in range(steps):
        hit = (position[None, :] == lengths[:, None] + step)[:, :, None]
        new_keys = jnp.where(hit, key_rows[:, step][:, None, :], new_keys)
        new_values = jnp.where(hit, value_rows[:, step][:, None, :], new_values)
    query_heads = query.reshape(group, steps, HEADS, HEAD)
    key_heads = new_keys.reshape(group, slots, HEADS, HEAD)
    value_heads = new_values.reshape(group, slots, HEADS, HEAD)
    scores = jnp.einsum(
        "rthd,rshd->rths", query_heads, key_heads, preferred_element_type=jnp.float32
    ) * HEAD ** (-0.5)
    limit = lengths[:, None] + jnp.arange(steps, dtype=jnp.int32)[None, :]
    valid = position[None, None, None, :] <= limit[:, :, None, None]
    masked = jnp.where(valid, scores, -1e30)
    peak = jnp.max(masked, axis=-1)
    expo = jnp.where(valid, jnp.exp(masked - peak[..., None]), 0.0)
    total = jnp.sum(expo, axis=-1)
    partial_value = jnp.einsum(
        "rths,rshd->rthd",
        expo.astype(jnp.bfloat16),
        value_heads,
        preferred_element_type=jnp.float32,
    )
    peak, total, partial_value = merged((peak, total, partial_value), "seq", combine)
    attn = (partial_value / total[..., None]).reshape(group, steps, width).astype(jnp.bfloat16)
    out_part = (jnp.dot(attn, full_out, preferred_element_type=jnp.float32) + b_out).astype(
        jnp.bfloat16
    )
    projected = lax.all_gather(out_part, "seq", axis=2, tiled=True)
    mid = residual + projected.astype(jnp.float32)
    normed2 = layer_norm(mid, norm2_gain, norm2_bias).astype(jnp.bfloat16)
    hidden = jax.nn.gelu(
        jnp.dot(normed2, full_up, preferred_element_type=jnp.float32) + b_up, approximate=False
    ).astype(jnp.bfloat16)
    feed = jnp.dot(
        hidden,
        lax.all_gather(w_down, "req", axis=1, tiled=True),
        preferred_element_type=jnp.float32,
    )
    summed = lax.psum(feed.astype(jnp.bfloat16), "seq").astype(jnp.float32)
    hidden_out = (mid + summed + b_down).astype(jnp.bfloat16)
    return (hidden_out, new_keys, new_values)


def solution(mesh):
    in_specs = (
        P("req", None, None),
        P("req"),
        P("req", "seq", None),
        P("req", "seq", None),
        P(),
        P(),
        P("req", "seq"),
        P("seq"),
        P("req", "seq"),
        P("seq"),
        P("req", "seq"),
        P("seq"),
        P("req", "seq"),
        P("seq"),
        P(),
        P(),
        P("req", "seq"),
        P("seq"),
        P("seq", "req"),
        P(),
    )
    out_specs = (P("req", None, None), P("req", "seq", None), P("req", "seq", None))
    return jax.shard_map(body, mesh=mesh, in_specs=in_specs, out_specs=out_specs, check_vma=False)
```

profile of v0, /device:TPU:2, one launch (start us, length us, event | category | flops | bytes accessed | tf_op | source)
XLA Modules:
  0.0 581.9 jit_solution(13199156575693389009)
XLA Ops:
  10.8 13.6 %all_gather.50 = bf16[2048,64]{0,1:T(8,128)(2,1)S(1)} all-gather(bf16[256,64]{0,1:T(8,128)(2,1)} %param.32), channel_id=1, replica_groups=mesh['seq'=32,'req'=8] {'req'}, dimensions={0}, use_global_device_ids=true | all-gather | bytes 294912 | tf_op jit(solution)/shard_map/all_gather | solution.py:70
  24.4 1.2 fusion.26
  25.7 54.4 %all_gather.51 = bf16[8,4,2048]{0,1,2:T(4,128)(2,1)S(1)} all-gather(bf16[8,4,64]{0,1,2:T(4,128)(2,1)S(1)} %copy.89), channel_id=1, replica_groups=mesh['seq'=32,'req'=8] {'seq'}, dimensions={2}, use_global_device_ids=true | all-gather | bytes 135168 | tf_op jit(solution)/shard_map/all_gather | solution.py:86
  80.1 3.8 fusion.133
  83.9 2.2 copy.105
  87.7 12.8 %all_gather.44 = bf16[2048,64]{0,1:T(8,128)(2,1)S(1)} all-gather(bf16[256,64]{0,1:T(8,128)(2,1)S(1)} %copy-done.3), channel_id=1, replica_groups=mesh['seq'=32,'req'=8] {'req'}, dimensions={0}, use_global_device_ids=true | all-gather | bytes 294912 | tf_op jit(solution)/shard_map/all_gather | solution.py:69
  100.9 50.0 %all_gather.45 = bf16[8,4,2048]{0,1,2:T(4,128)(2,1)S(1)} all-gather(bf16[8,4,64]{0,1,2:T(4,128)(2,1)S(1)} %copy.76), channel_id=1, replica_groups=mesh['seq'=32,'req'=8] {'seq'}, dimensions={2}, use_global_device_ids=true | all-gather | bytes 135168 | tf_op jit(solution)/shard_map/all_gather | solution.py:85
  151.0 3.8 fusion.134
  154.8 2.2 copy.101
  158.5 12.8 %all_gather.46 = bf16[2048,64]{0,1:T(8,128)(2,1)S(1)} all-gather(bf16[256,64]{0,1:T(8,128)(2,1)S(1)} %copy-done.4), channel_id=1, replica_groups=mesh['seq'=32,'req'=8] {'req'}, dimensions={0}, use_global_device_ids=true | all-gather | bytes 294912 | tf_op jit(solution)/shard_map/all_gather | solution.py:68
  171.7 50.1 %all_gather.47 = bf16[8,4,2048]{0,1,2:T(4,128)(2,1)S(1)} all-gather(bf16[8,4,64]{0,1,2:T(4,128)(2,1)S(1)} %copy.81), channel_id=1, replica_groups=mesh['seq'=32,'req'=8] {'seq'}, dimensions={2}, use_global_device_ids=true | all-gather | bytes 135168 | tf_op jit(solution)/shard_map/all_gather | solution.py:84
  223.0 2.9 select_select_fusion
  226.0 1.3 fusion.135
  231.1 47.5 %all-gather.1 = bf16[256,4,16]{2,1,0:T(4,128)(2,1)S(1)} all-gather(bf16[8,4,16]{2,1,0:T(4,128)(2,1)S(1)} %copy.88), channel_id=3, replica_groups=mesh['seq'=32,'req'=8] {'seq'}, dimensions={0}, use_global_device_ids=true | all-gather | bytes 33792 | tf_op jit(solution)/shard_map/all_gather | solution.py:12
  278.6 47.5 %all-gather = bf16[256,4,16]{2,1,0:T(4,128)(2,1)S(1)} all-gather(bf16[8,4,16]{2,1,0:T(4,128)(2,1)S(1)} %copy.86), channel_id=2, replica_groups=mesh['seq'=32,'req'=8] {'seq'}, dimensions={0}, use_global_device_ids=true | all-gather | bytes 33792 | tf_op jit(solution)/shard_map/all_gather | solution.py:12
  326.1 12.8 %all_gather.54 = bf16[2048,64]{0,1:T(8,128)(2,1)S(1)} all-gather(bf16[256,64]{0,1:T(8,128)(2,1)S(1)} %copy-done.5), channel_id=1, replica_groups=mesh['seq'=32,'req'=8] {'req'}, dimensions={0}, use_global_device_ids=true | all-gather | bytes 294912 | tf_op jit(solution)/shard_map/all_gather | solution.py:71
  339.9 38.4 %while.19 = (s32[]{:T(128)}, f32[8,4,16]{2,1,0:T(4,128)S(1)}, f32[8,4,16]{2,1,0:T(4,128)S(1)}, f32[8,4,16,128]{3,2,1,0:T(8,128)S(1)}, bf16[32,8,4,16]{3,2,1,0:T(...) while((s32[]{:T(128)}, f32[8,4,16]{2,1,0:T(4,128)S(1)}, ...), condition=%wide.region_5.6_spmd, body=%wide.region_4.5_spmd.sunk | while | flops 266245 | bytes 673943 | solution.py:20
  339.9 1.2 fusion.143
  341.2 1.2 fusion.143
  346.1 1.2 fusion.143
  347.4 1.2 fusion.143
  348.6 1.2 fusion.143
  351.1 1.2 fusion.143
  352.3 1.2 fusion.143
  353.5 1.2 fusion.143
  357.3 1.2 fusion.143
  359.8 1.2 fusion.143
  361.0 1.2 fusion.143
  378.8 50.4 %all_gather.55 = bf16[8,4,2048]{0,1,2:T(4,128)(2,1)S(1)} all-gather(bf16[8,4,64]{0,1,2:T(4,128)(2,1)S(1)} %copy.96), channel_id=1, replica_groups=mesh['seq'=32,'req'=8] {'seq'}, dimensions={2}, use_global_device_ids=true | all-gather | bytes 135168 | tf_op jit(solution)/shard_map/all_gather | solution.py:120
  430.9 1.6 fusion.94
  432.5 2.2 convolution_convert_fusion
  434.7 138.8 %all-reduce.2.cloned.1.call-done = bf16[8,4,2048]{2,0,1:T(8,128)(2,1)} async-done(((bf16[8,4,2048]{2,0,1:T(8,128)(2,1)}), bf16[8,4,2048]{2,0,1:T(8,128)(2,1)}) %all-reduce.2.cloned.1.call-update) | async-done | bytes 131088 | tf_op jit(solution)/shard_map/psum | solution.py:131
  (136 shorter events, 42.0 us)
Async XLA Ops:
  7.2 331.8 %all-gather.11.cloned.1.call-start = ((), (), s32[]{:S(2)}) async-start(), calls=%async_computation.3 | async-start | bytes 4325376 | tf_op jit(solution)/shard_map/all_gather | solution.py:12
  83.9 3.7 copy-start.3
  83.9 16.6 %copy-start = (bf16[8,4,2048]{2,1,0:T(4,128)(2,1)S(1)}, bf16[8,4,2048]{2,1,0:T(4,128)(2,1)}, u32[]{:S(2)}) copy-start(bf16[8,4,2048]{2,1,0:T(4,128)(2,1)} %param.22) | copy-start | bytes 393220
  83.9 16.6 %copy-start.11 = (f32[2048]{0:T(1024)S(1)}, f32[2048]{0:T(1024)}, u32[]{:S(2)}) copy-start(f32[2048]{0:T(1024)} %param.27) | copy-start | bytes 24580
  83.9 16.6 %copy-start.12 = (f32[2048]{0:T(1024)S(1)}, f32[2048]{0:T(1024)}, u32[]{:S(2)}) copy-start(f32[2048]{0:T(1024)} %param.26) | copy-start | bytes 24580
  83.9 16.6 %copy-start.13 = (f32[64]{0:T(128)S(1)}, f32[64]{0:T(128)}, u32[]{:S(2)}) copy-start(f32[64]{0:T(128)} %param.31) | copy-start | bytes 772
  154.8 3.7 copy-start.4
  154.8 16.5 %copy-start.14 = (f32[64]{0:T(128)S(1)}, f32[64]{0:T(128)}, u32[]{:S(2)}) copy-start(f32[64]{0:T(128)} %param.29) | copy-start | bytes 772
  171.7 51.2 %copy-start.9 = (s32[8]{0:T(128)S(1)}, s32[8]{0:T(128)}, u32[]{:S(2)}) copy-start(s32[8]{0:T(128)} %param.23) | copy-start | bytes 100
  226.0 2.0 copy-start.1
  226.0 2.0 copy-start.2
  227.2 98.8 %copy-start.5 = (bf16[256,64]{0,1:T(8,128)(2,1)S(1)}, bf16[256,64]{0,1:T(8,128)(2,1)}, u32[]{:S(2)}) copy-start(bf16[256,64]{0,1:T(8,128)(2,1)} %param.34) | copy-start | bytes 98308
  228.7 202.2 %all-gather.7.cloned.1.call-start = ((), (), s32[]{:S(2)}) async-start(), calls=%async_computation | async-start | bytes 1179648 | tf_op jit(solution)/shard_map/all_gather | solution.py:72
  229.5 203.0 %all-gather.9.cloned.1.call-start = ((), (), s32[]{:S(2)}) async-start(), calls=%async_computation.1 | async-start | bytes 1179648 | tf_op jit(solution)/shard_map/all_gather | solution.py:128
  230.2 343.4 %all-reduce.2.cloned.1.call-start = ((), (), s32[]{:S(2)}) async-start(), calls=%async_computation.2 | async-start | bytes 262144 | tf_op jit(solution)/shard_map/psum | solution.py:131
  339.9 38.6 %copy-start.15 = (f32[64]{0:T(128)S(1)}, f32[64]{0:T(128)}, u32[]{:S(2)}) copy-start(f32[64]{0:T(128)} %param.35) | copy-start | bytes 772
  378.8 52.1 %copy-start.6 = (f32[2048]{0:T(1024)S(1)}, f32[2048]{0:T(1024)}, u32[]{:S(2)}) copy-start(f32[2048]{0:T(1024)} %param.37) | copy-start | bytes 24580
  378.8 52.1 %copy-start.7 = (f32[2048]{0:T(1024)S(1)}, f32[2048]{0:T(1024)}, u32[]{:S(2)}) copy-start(f32[2048]{0:T(1024)} %param.36) | copy-start | bytes 24580
  378.8 52.1 %copy-start.10 = (f32[256]{0:T(256)S(1)}, f32[256]{0:T(256)}, u32[]{:S(2)}) copy-start(f32[256]{0:T(256)} %param.39) | copy-start | bytes 3076
  430.4 143.1 %copy-start.8 = (f32[2048]{0:T(1024)S(1)}, f32[2048]{0:T(1024)}, u32[]{:S(2)}) copy-start(f32[2048]{0:T(1024)} %param.41) | copy-start | bytes 24580
Sparse Core Ops, SparseCore 0:
  228.8 78.4 all-gather.10
  309.2 24.8 all-gather.6
  335.9 25.9 all-gather.8
  434.9 138.6 all-reduce.1
where the time goes:
time: 583 us; the launch traced here: 582 us
  blocking collectives  352 us (60%)
  waiting for transfers between devices  140 us (24%)
  other arithmetic  47.2 us (8%)
  local copies, waits for them, and re-layouts  19.5 us (3%)
  between operations  14.1 us (2%)
  matrix products  7.72 us (1%)
    psum x1, waiting for transfers between devices, body(): summed = lax.psum(feed.astype(jnp.bfloat16), 'seq').astype(jnp.float32)  139 us
    all_gather x2, blocking collectives, merged(): lax.all_gather(part.astype(kind), axis)  94.9 us
    all_gather x1, blocking collectives, body(): lax.all_gather(value_cols, 'seq', axis=2, tiled=True)  54.4 us
    all_gather x1, blocking collectives, body(): projected = lax.all_gather(out_part, 'seq', axis=2, tiled=True)  50.4 us
    all_gather x1, blocking collectives, body(): lax.all_gather(query_cols, 'seq', axis=2, tiled=True)  50.1 us
    all_gather x1, blocking collectives, body(): lax.all_gather(key_cols, 'seq', axis=2, tiled=True)  50 us
    add x31, other arithmetic, combine(): part = part_a * scale_a[..., None] + part_b * scale_b[..., None]  36.3 us
    all_gather x1, blocking collectives, body(): lax.all_gather(w_value, 'req', axis=0, tiled=True)  13.6 us
  transfers between devices with their start and end apart: 4, of which 1 were waited for; matrix products, arithmetic and copies ran while one was open for 7% of the time, Pallas kernels for 0%

commit v1 on v0

--- a/solution.py
+++ b/solution.py
@@ -5,6 +5,11 @@
 
 HEADS = 16
 HEAD = 128
+
+
+def mark_side_here(t0):
+    piece_next = lax.all_gather(t0, axis_name="seq").sum(axis=0)
+    return piece_next
 
 
 def merged(x, axis, combine):
@@ -128,7 +133,7 @@
         lax.all_gather(w_down, "req", axis=1, tiled=True),
         preferred_element_type=jnp.float32,
     )
-    summed = lax.psum(feed.astype(jnp.bfloat16), "seq").astype(jnp.float32)
+    summed = mark_side_here(feed.astype(jnp.bfloat16)).astype(jnp.float32)
     hidden_out = (mid + summed + b_down).astype(jnp.bfloat16)
     return (hidden_out, new_keys, new_values)
 

time: 583 us -> 526 us (0.902)
  waiting for transfers between devices: 140 us -> 80 us
    psum x1 -> x0, waiting for transfers between devices: 139 us -> none  [body(): summed = lax.psum(feed.astype(jnp.bfloat16), 'seq').astype(jnp.float32)]
    all_gather x0 -> x1, waiting for transfers between devices: none -> 78.5 us  [mark_side_here(): piece_next = lax.all_gather(t0, axis_name='seq').sum(axis=0)]
  transfers between devices with their start and end apart: 4 -> 4, of which waited for: 1 -> 1; matrix products, arithmetic and copies ran while one was open for 7% -> 8% of each run, Pallas kernels for 0% -> 0%
where the time goes in v1:
time: 526 us; the launch traced here: 524 us
  blocking collectives  352 us (67%)
  waiting for transfers between devices  80 us (15%)
  other arithmetic  49.2 us (9%)
  local copies, waits for them, and re-layouts  19.5 us (4%)
  between operations  14.1 us (3%)
  matrix products  7.72 us (1%)
    all_gather x2, blocking collectives, merged(): lax.all_gather(part.astype(kind), axis)  94.9 us
    all_gather x1, waiting for transfers between devices, mark_side_here(): piece_next = lax.all_gather(t0, axis_name='seq').sum(axis=0)  78.5 us
    all_gather x1, blocking collectives, body(): lax.all_gather(value_cols, 'seq', axis=2, tiled=True)  54.4 us
    all_gather x1, blocking collectives, body(): projected = lax.all_gather(out_part, 'seq', axis=2, tiled=True)  50.4 us
    all_gather x1, blocking collectives, body(): lax.all_gather(query_cols, 'seq', axis=2, tiled=True)  50.1 us
    all_gather x1, blocking collectives, body(): lax.all_gather(key_cols, 'seq', axis=2, tiled=True)  50 us
    add x31, other arithmetic, combine(): part = part_a * scale_a[..., None] + part_b * scale_b[..., None]  36.3 us
    all_gather x1, blocking collectives, body(): lax.all_gather(w_value, 'req', axis=0, tiled=True)  13.6 us
  transfers between devices with their start and end apart: 4, of which 1 were waited for; matrix products, arithmetic and copies ran while one was open for 8% of the time, Pallas kernels for 0%

profile of v1, /device:TPU:2, one launch (start us, length us, event | category | flops | bytes accessed | tf_op | source)
XLA Modules:
  0.0 523.6 jit_solution(743119763912550425)
XLA Ops:
  10.8 13.6 %all_gather.56 = bf16[2048,64]{0,1:T(8,128)(2,1)S(1)} all-gather(bf16[256,64]{0,1:T(8,128)(2,1)} %param.32), channel_id=1, replica_groups=mesh['seq'=32,'req'=8] {'req'}, dimensions={0}, use_global_device_ids=true | all-gather | bytes 294912 | tf_op jit(solution)/shard_map/all_gather | solution.py:75
  24.4 1.2 fusion.26
  25.7 54.4 %all_gather.57 = bf16[8,4,2048]{0,1,2:T(4,128)(2,1)S(1)} all-gather(bf16[8,4,64]{0,1,2:T(4,128)(2,1)S(1)} %copy.117), channel_id=1, replica_groups=mesh['seq'=32,'req'=8] {'seq'}, dimensions={2}, use_global_device_ids=true | all-gather | bytes 135168 | tf_op jit(solution)/shard_map/all_gather | solution.py:91
  80.1 3.8 fusion.133
  83.9 2.2 copy.133
  87.7 12.8 %all_gather.50 = bf16[2048,64]{0,1:T(8,128)(2,1)S(1)} all-gather(bf16[256,64]{0,1:T(8,128)(2,1)S(1)} %copy-done.3), channel_id=1, replica_groups=mesh['seq'=32,'req'=8] {'req'}, dimensions={0}, use_global_device_ids=true | all-gather | bytes 294912 | tf_op jit(solution)/shard_map/all_gather | solution.py:74
  100.9 50.0 %all_gather.51 = bf16[8,4,2048]{0,1,2:T(4,128)(2,1)S(1)} all-gather(bf16[8,4,64]{0,1,2:T(4,128)(2,1)S(1)} %copy.104), channel_id=1, replica_groups=mesh['seq'=32,'req'=8] {'seq'}, dimensions={2}, use_global_device_ids=true | all-gather | bytes 135168 | tf_op jit(solution)/shard_map/all_gather | solution.py:90
  151.0 3.8 fusion.134
  154.8 2.2 copy.129
  158.5 12.8 %all_gather.52 = bf16[2048,64]{0,1:T(8,128)(2,1)S(1)} all-gather(bf16[256,64]{0,1:T(8,128)(2,1)S(1)} %copy-done.4), channel_id=1, replica_groups=mesh['seq'=32,'req'=8] {'req'}, dimensions={0}, use_global_device_ids=true | all-gather | bytes 294912 | tf_op jit(solution)/shard_map/all_gather | solution.py:73
  171.7 50.1 %all_gather.53 = bf16[8,4,2048]{0,1,2:T(4,128)(2,1)S(1)} all-gather(bf16[8,4,64]{0,1,2:T(4,128)(2,1)S(1)} %copy.109), channel_id=1, replica_groups=mesh['seq'=32,'req'=8] {'seq'}, dimensions={2}, use_global_device_ids=true | all-gather | bytes 135168 | tf_op jit(solution)/shard_map/all_gather | solution.py:89
  223.0 2.9 select_select_fusion
  226.0 1.3 fusion.135
  231.1 47.4 %all-gather.1 = bf16[256,4,16]{2,1,0:T(4,128)(2,1)S(1)} all-gather(bf16[8,4,16]{2,1,0:T(4,128)(2,1)S(1)} %copy.116), channel_id=3, replica_groups=mesh['seq'=32,'req'=8] {'seq'}, dimensions={0}, use_global_device_ids=true | all-gather | bytes 33792 | tf_op jit(solution)/shard_map/all_gather | solution.py:17
  278.6 47.5 %all-gather = bf16[256,4,16]{2,1,0:T(4,128)(2,1)S(1)} all-gather(bf16[8,4,16]{2,1,0:T(4,128)(2,1)S(1)} %copy.114), channel_id=2, replica_groups=mesh['seq'=32,'req'=8] {'seq'}, dimensions={0}, use_global_device_ids=true | all-gather | bytes 33792 | tf_op jit(solution)/shard_map/all_gather | solution.py:17
  326.1 12.8 %all_gather.60 = bf16[2048,64]{0,1:T(8,128)(2,1)S(1)} all-gather(bf16[256,64]{0,1:T(8,128)(2,1)S(1)} %copy-done.5), channel_id=1, replica_groups=mesh['seq'=32,'req'=8] {'req'}, dimensions={0}, use_global_device_ids=true | all-gather | bytes 294912 | tf_op jit(solution)/shard_map/all_gather | solution.py:76
  339.9 38.4 %while.19 = (s32[]{:T(128)}, f32[8,4,16]{2,1,0:T(4,128)S(1)}, f32[8,4,16]{2,1,0:T(4,128)S(1)}, f32[8,4,16,128]{3,2,1,0:T(8,128)S(1)}, bf16[32,8,4,16]{3,2,1,0:T(...) while((s32[]{:T(128)}, f32[8,4,16]{2,1,0:T(4,128)S(1)}, ...), condition=%wide.region_5.6_spmd, body=%wide.region_4.5_spmd.sunk | while | flops 266245 | bytes 673943 | solution.py:25
  342.4 1.2 fusion.143
  343.7 1.2 fusion.143
  346.1 1.2 fusion.143
  347.4 1.2 fusion.143
  348.6 1.2 fusion.143
  352.3 1.2 fusion.143
  353.6 1.2 fusion.143
  357.3 1.2 fusion.143
  359.8 1.2 fusion.143
  361.0 1.2 fusion.143
  378.9 50.4 %all_gather.61 = bf16[8,4,2048]{0,1,2:T(4,128)(2,1)S(1)} all-gather(bf16[8,4,64]{0,1,2:T(4,128)(2,1)S(1)} %copy.124), channel_id=1, replica_groups=mesh['seq'=32,'req'=8] {'seq'}, dimensions={2}, use_global_device_ids=true | all-gather | bytes 135168 | tf_op jit(solution)/shard_map/all_gather | solution.py:125
  430.9 1.6 fusion.94
  432.5 2.2 convolution_convert_fusion
  434.7 78.5 %all-gather.15.cloned.1.call-done = bf16[256,4,2048]{2,0,1:T(8,128)(2,1)} async-done(((bf16[8,4,2048]{2,0,1:T(8,128)(2,1)}), bf16[256,4,2048]{2,0,1:T(8,128)(2,1)}) %all-gather.15.cloned.1.call-update) | async-done | bytes 4194320 | tf_op jit(solution)/shard_map/all_gather | solution.py:11
  513.3 2.9 bitcast_reduce_fusion
  (137 shorter events, 42.2 us)
Async XLA Ops:
  7.2 331.8 %all-gather.13.cloned.1.call-start = ((), (), s32[]{:S(2)}) async-start(), calls=%async_computation.2 | async-start | bytes 4325376 | tf_op jit(solution)/shard_map/all_gather | solution.py:17
  83.9 3.7 copy-start.3
  83.9 16.6 %copy-start = (bf16[8,4,2048]{2,1,0:T(4,128)(2,1)S(1)}, bf16[8,4,2048]{2,1,0:T(4,128)(2,1)}, u32[]{:S(2)}) copy-start(bf16[8,4,2048]{2,1,0:T(4,128)(2,1)} %param.22) | copy-start | bytes 393220
  83.9 16.6 %copy-start.11 = (f32[2048]{0:T(1024)S(1)}, f32[2048]{0:T(1024)}, u32[]{:S(2)}) copy-start(f32[2048]{0:T(1024)} %param.27) | copy-start | bytes 24580
  83.9 16.6 %copy-start.12 = (f32[2048]{0:T(1024)S(1)}, f32[2048]{0:T(1024)}, u32[]{:S(2)}) copy-start(f32[2048]{0:T(1024)} %param.26) | copy-start | bytes 24580
  83.9 16.6 %copy-start.13 = (f32[64]{0:T(128)S(1)}, f32[64]{0:T(128)}, u32[]{:S(2)}) copy-start(f32[64]{0:T(128)} %param.31) | copy-start | bytes 772
  154.8 3.7 copy-start.4
  154.8 16.5 %copy-start.14 = (f32[64]{0:T(128)S(1)}, f32[64]{0:T(128)}, u32[]{:S(2)}) copy-start(f32[64]{0:T(128)} %param.29) | copy-start | bytes 772
  171.7 51.2 %copy-start.9 = (s32[8]{0:T(128)S(1)}, s32[8]{0:T(128)}, u32[]{:S(2)}) copy-start(s32[8]{0:T(128)} %param.23) | copy-start | bytes 100
  226.0 2.0 copy-start.1
  226.0 2.0 copy-start.2
  227.2 98.8 %copy-start.5 = (bf16[256,64]{0,1:T(8,128)(2,1)S(1)}, bf16[256,64]{0,1:T(8,128)(2,1)}, u32[]{:S(2)}) copy-start(bf16[256,64]{0,1:T(8,128)(2,1)} %param.34) | copy-start | bytes 98308
  228.7 202.1 %all-gather.9.cloned.1.call-start = ((), (), s32[]{:S(2)}) async-start(), calls=%async_computation | async-start | bytes 1179648 | tf_op jit(solution)/shard_map/all_gather | solution.py:77
  229.5 203.0 %all-gather.11.cloned.1.call-start = ((), (), s32[]{:S(2)}) async-start(), calls=%async_computation.1 | async-start | bytes 1179648 | tf_op jit(solution)/shard_map/all_gather | solution.py:133
  230.2 283.1 %all-gather.15.cloned.1.call-start = ((), (), s32[]{:S(2)}) async-start(), calls=%async_computation.3 | async-start | bytes 4325376 | tf_op jit(solution)/shard_map/all_gather | solution.py:11
  339.9 38.6 %copy-start.15 = (f32[64]{0:T(128)S(1)}, f32[64]{0:T(128)}, u32[]{:S(2)}) copy-start(f32[64]{0:T(128)} %param.35) | copy-start | bytes 772
  378.8 52.1 %copy-start.6 = (f32[2048]{0:T(1024)S(1)}, f32[2048]{0:T(1024)}, u32[]{:S(2)}) copy-start(f32[2048]{0:T(1024)} %param.37) | copy-start | bytes 24580
  378.8 52.1 %copy-start.7 = (f32[2048]{0:T(1024)S(1)}, f32[2048]{0:T(1024)}, u32[]{:S(2)}) copy-start(f32[2048]{0:T(1024)} %param.36) | copy-start | bytes 24580
  378.8 52.0 %copy-start.10 = (f32[256]{0:T(256)S(1)}, f32[256]{0:T(256)}, u32[]{:S(2)}) copy-start(f32[256]{0:T(256)} %param.39) | copy-start | bytes 3076
  434.7 81.4 %copy-start.8 = (f32[2048]{0:T(1024)S(1)}, f32[2048]{0:T(1024)}, u32[]{:S(2)}) copy-start(f32[2048]{0:T(1024)} %param.41) | copy-start | bytes 24580
Sparse Core Ops, SparseCore 0:
  228.8 78.4 all-gather.12
  309.2 24.8 all-gather.8
  335.9 25.9 all-gather.10
  434.9 78.3 all-gather.14
